TPU v7x, 256 devices: a whole 4x4x8 slice. The times are simulated.
256 devices in a mesh: strike: 16 (over z, core), dip: 4 (over x), depth: 4 (over y).
Axes of the slice: x: 4, y: 4, z: 8, core: 2. Of those that a mesh axis runs over, the one named last changes fastest.
Arguments:
- state: float32 [20, 27, 131072], P(None, None, ('strike', 'dip', 'depth')), may hold values from -6 to 6
- geometry: float32 [3, 3, 131072], P(None, None, ('strike', 'dip', 'depth')), may hold values from -3 to 3
- normals: float32 [4, 3, 131072], P(None, None, ('strike', 'dip', 'depth')), may hold values from -3 to 3
- wave_speed: float32 [131072], P(('strike', 'dip', 'depth')), may hold values from 0.5 to 2
- cluster: int32 [131072], P(('strike', 'dip', 'depth')), may hold values 0 or 1
- nb_index: int32 [4, 131072], P(None, ('strike', 'dip', 'depth')), may hold values from 0 to 1535, as said below
- nb_face: int32 [4, 131072], P(None, ('strike', 'dip', 'depth')), may hold values from 0 to 3, as said below
- orientation: int32 [4, 131072], P(None, ('strike', 'dip', 'depth')), may hold values from 0 to 2
- export_strike: int32 [2, 65536], P(None, ('strike', 'dip', 'depth')), may hold values from 0 to 2047, as said below
- export_dip: int32 [2, 32768], P(None, ('strike', 'dip', 'depth')), may hold values from 0 to 2047, as said below
- export_depth: int32 [2, 32768], P(None, ('strike', 'dip', 'depth')), may hold values from 0 to 2047, as said below
- stiffness: float32 [3, 20, 20], replicated, may hold values from -1.25 to 1.25
- stiff_volume: float32 [3, 20, 20], replicated, may hold values from -1.25 to 1.25
- jacobians: float32 [3, 27, 27], replicated, may hold values from -0.625 to 0.625
- face_proj: float32 [4, 10, 20], replicated, may hold values from -1.25 to 1.25
- face_lift: float32 [4, 20, 10], replicated, may hold values from -1 to 1
- rotations: float32 [3, 10, 10], replicated, may hold values from -2 to 2
Outputs:
- new_state: float32 [20, 27, 131072], P(None, None, ('strike', 'dip', 'depth'))
Inputs may be any that keep to these rules, and one draw needn't show every extreme that they name: `nb_index`: each face is paired with exactly one face: values below 512 name a local element, larger ones a row of the received face blocks as the steps order them; every used row belongs to a linked face, and the link counts reach 256 and 128. `nb_face`: the neighbour's face number of the pairing in nb_index. `export_strike`: entry l names the local face slot of link l to that neighbour; slots beyond a link count hold 0 and are never referred to; some device uses all 256. `export_dip`: as export_strike, with at most 128 links a neighbour. `export_depth`: as export_strike, with at most 128 links a neighbour.
All inputs are finite; a program needn't handle non-finite values. No bound on the sum of `cluster` on one device may be relied on, other than what follows from the above.
Results may differ from a plain program's by a relative error of at most 0.0003.
Values sent between devices are 32-bit elements; how exact they have to be, the bound alone decides.
A program may use at most 128 MiB of HBM per device.

v0:
```python
import functools
import math

import jax
import jax.numpy as jnp
from jax import lax
from jax.experimental import pallas as pl
from jax.experimental.pallas import tpu as pltpu
from jax.sharding import PartitionSpec as P

MESH = pl.DeviceIdType.MESH
BASIS, QUANT, FACE = 20, 27, 10
ELEM = 512
TIME_STEP = 0.5
ORDER = 4
WIDE = 256
ROWS = 3
TRACE = 272
f32, bf16, i32 = jnp.float32, jnp.bfloat16, jnp.int32

LINKS = (
    ("strike", 0, 256),
    ("strike", 256, 256),
    ("dip", 512, 128),
    ("dip", 640, 128),
    ("depth", 768, 128),
    ("depth", 896, 128),
)


def dot(a, b):
    return jnp.dot(a, b, preferred_element_type=f32)


def split(x):
    high = x.astype(bf16)
    return high, (x - high.astype(f32)).astype(bf16)


def rep8(m):
    n, k = m.shape
    return jnp.broadcast_to(m[:, None, :], (n, 8, k)).reshape(n * 8, k)


def iota(shape, dim):
    return lax.broadcasted_iota(i32, shape, dim)


def spread(m, parts, count, first_part, last_part):
    n, k = m.shape
    width = parts * count * 8
    col = iota((k, width), 1)
    row = iota((k, width), 0)
    put = jnp.zeros((k, width), jnp.bool_)
    for part in range(first_part, last_part + 1):
        put = put | ((col - part * count * 8) >> 3 == row)
    wide = dot(rep8(m.astype(f32)).astype(bf16), jnp.where(put, 1.0, 0.0).astype(bf16))
    same = (iota((n * 8, width), 0) & 7) == (iota((n * 8, width), 1) & 7)
    return jnp.where(same, wide, 0.0)


def stacked(m, count):
    high, low = split(m)
    return (spread(high, 3, count, 0, 1) + spread(low, 3, count, 2, 2)).astype(bf16)


def jacobian_weights(jac_ref, tmp_ref, out_ref):
    tmp_ref[...] = jnp.zeros((128, 128), f32)
    for j in range(3):
        high, low = split(jac_ref[j])
        at = slice(32 * j, 32 * j + QUANT)
        tmp_ref[0:QUANT, at] = high.astype(f32)
        tmp_ref[32 : 32 + QUANT, at] = high.astype(f32)
        tmp_ref[64 : 64 + QUANT, at] = low.astype(f32)
    out_ref[...] = tmp_ref[...].T[:96, :96].astype(bf16)


def stiff_weights(mat_ref, sign, high_ref, low_ref):
    high_sum = jnp.zeros((160, 480), f32)
    low_sum = jnp.zeros((160, 480), f32)
    for d in range(3):
        high, low = split(sign * mat_ref[d])
        high_sum = high_sum + spread(high, 3, BASIS, d, d)
        low_sum = low_sum + spread(low, 3, BASIS, d, d)
    high_ref[...] = high_sum.astype(bf16)
    low_ref[...] = low_sum.astype(bf16)


def packed_project(m):
    high, low = split(m)
    row = iota((32, FACE), 0)
    third = (row * 171) >> 9
    pick = jnp.where(third == iota((32, FACE), 1), 1.0, 0.0).astype(bf16)
    total = jnp.zeros((32, 480), f32)
    for part_from, part_to, piece in ((0, 1, high), (2, 2, low)):
        rows = dot(pick, piece).astype(bf16)
        col = iota((BASIS, 480), 1)
        put = jnp.zeros((BASIS, 480), jnp.bool_)
        for part in range(part_from, part_to + 1):
            put = put | ((col - part * 160) >> 3 == iota((BASIS, 480), 0))
        total = total + dot(rows, jnp.where(put, 1.0, 0.0).astype(bf16))
    out_row = iota((32, 480), 0)
    same = (out_row - 3 * ((out_row * 171) >> 9)) == (iota((32, 480), 1) & 7)
    return jnp.where(same & (out_row < 30), total, 0.0).astype(bf16)


def packed_rotate(m):
    high, low = split(m)
    total = jnp.zeros((80, 96), f32)
    col = iota((FACE, 96), 1)
    for part_from, part_to, piece in ((0, 1, high), (2, 2, low)):
        put = jnp.zeros((FACE, 96), jnp.bool_)
        for part in range(part_from, part_to + 1):
            inner = col - part * 32
            put = put | ((inner >= 0) & (inner < 30) & ((inner * 171) >> 9 == iota((FACE, 96), 0)))
        total = total + dot(rep8(piece.astype(f32)).astype(bf16), jnp.where(put, 1.0, 0.0).astype(bf16))
    inner = iota((80, 96), 1) & 31
    same = (inner - 3 * ((inner * 171) >> 9)) == (iota((80, 96), 0) & 7)
    return jnp.where(same, total, 0.0).astype(bf16)


def mixed(field, geo, weights):
    high, low = split(field)
    moved = dot(weights, jnp.concatenate([high, low, high], axis=0))
    n = field.shape[1]
    parts = [moved[32 * j : 32 * j + 32].reshape(4, 8, n) for j in range(3)]
    return [
        (geo[d][0] * parts[0] + geo[d][1] * parts[1] + geo[d][2] * parts[2]).reshape(32, n)
        for d in range(3)
    ]


def transport(load, geo, jac_ref, high_ref, low_ref, mix_ref):
    for b in range(BASIS):
        for d, rows in enumerate(mixed(load(b), geo, jac_ref[...])):
            for s in range(4):
                at = (d * BASIS + b) * 8
                mix_ref[s, at : at + 8, :] = rows[8 * s : 8 * s + 8]
    slabs = []
    for s in range(4):
        high, low = split(mix_ref[s])
        weights_high = high_ref[...]
        slabs.append(dot(weights_high, high) + dot(weights_high, low) + dot(low_ref[...], high))
    return slabs


def kernel(
    remote,
    state_ref,
    geo_ref,
    nrm_ref,
    speed_ref,
    cluster_ref,
    nbi_ref,
    nbf_ref,
    orient_ref,
    exs_ref,
    exd_ref,
    exz_ref,
    stiff_ref,
    vol_ref,
    jac_ref,
    proj_ref,
    lift_ref,
    rot_ref,
    out_ref,
    field,
    integral,
    mix,
    own,
    total,
    mine,
    pool,
    ship,
    near,
    cols_v,
    cols_s,
    tmp,
    w_jac,
    w_stiff_h,
    w_stiff_l,
    w_vol_h,
    w_vol_l,
    w_proj,
    w_proj3,
    w_rot,
    w_rot3,
    w_lift,
    cols_sem,
    send_sem,
    recv_sem,
):
    links = []
    for at, (axis, first, rows) in enumerate(LINKS):
        step = -1 if at % 2 == 0 else 1
        if remote:
            pos, count = lax.axis_index(axis), lax.axis_size(axis)
            there = pos > 0 if step < 0 else pos < count - 1
            target = jnp.clip(pos + step, 0, count - 1)
        else:
            there, target = True, None
        land = first + rows if step < 0 else first - rows
        links.append((axis, step, there, target, first, land, rows))

    if remote:
        barrier = pltpu.get_barrier_semaphore()
        greeted = 0
        for axis, step, there, target, *_ in links:

            @pl.when(there)
            def _(axis=axis, target=target):
                pl.semaphore_signal(barrier, inc=1, device_id={axis: target}, device_id_type=MESH)

            greeted = greeted + there.astype(i32)

    index = nbi_ref[...]
    cols_v[...] = ROWS * jnp.where(index < ELEM, nbf_ref[...] * ELEM + index, 3 * ELEM + index)
    cols_copy = pltpu.make_async_copy(cols_v, cols_s, cols_sem)
    cols_copy.start()

    jacobian_weights(jac_ref, tmp, w_jac)
    stiff_weights(stiff_ref, -1.0, w_stiff_h, w_stiff_l)
    for f in range(4):
        w_proj[80 * f : 80 * f + 80] = stacked(proj_ref[f], BASIS)
        w_proj3[32 * f : 32 * f + 32] = packed_project(proj_ref[f])

    zeros5 = jnp.zeros((5, WIDE), f32)

    def columns(h):
        return pl.ds(pl.multiple_of(h * WIDE, WIDE), WIDE)

    def geometry(h):
        return [
            [jnp.broadcast_to(geo_ref[d, j : j + 1, columns(h)], (8, WIDE))[None] for j in range(3)]
            for d in range(3)
        ]

    def time_weights(h):
        fine = cluster_ref[:, columns(h)] == 0
        rows = []
        for degree in range(ORDER):
            base = TIME_STEP ** (degree + 1) / math.factorial(degree + 1)
            coarse = base * (2.0 ** (degree + 1) - 1.0)
            rows.append(jnp.broadcast_to(jnp.where(fine, f32(base), f32(coarse)), (8, WIDE)))
        return rows

    def slab(ref, s, h):
        return ref[:, 8 * s : 8 * s + 8, columns(h)].reshape(BASIS * 8, WIDE)

    def predict(h, carry):
        cs = columns(h)
        geo, times = geometry(h), time_weights(h)
        for b in range(BASIS):
            value = jnp.concatenate([state_ref[b, :, cs], zeros5], axis=0)
            field[b, :, cs] = value
            integral[b, :, cs] = (times[0][None] * value.reshape(4, 8, WIDE)).reshape(32, WIDE)
        for degree in range(1, ORDER):
            slabs = transport(lambda b: field[b, :, cs], geo, w_jac, w_stiff_h, w_stiff_l, mix)
            for s in range(4):
                value = slabs[s].reshape(BASIS, 8, WIDE)
                if degree < ORDER - 1:
                    field[:, 8 * s : 8 * s + 8, cs] = value
                integral[:, 8 * s : 8 * s + 8, cs] += times[degree][None] * value
        for s in range(4):
            high, low = split(slab(integral, s, h))
            operand = jnp.concatenate([high, low, high], axis=0)
            traces = dot(w_proj[...], operand)
            for f in range(4):
                part = traces[80 * f : 80 * f + 80]
                own[f, :, 8 * s : 8 * s + 8, cs] = part.reshape(FACE, 8, WIDE)
            if s == 3:
                packed = dot(w_proj3[...], operand)
        for f in range(4):
            pieces = [
                own[f, :, 8 * s : 8 * s + 8, cs].reshape(80, WIDE) for s in range(3)
            ] + [packed[32 * f : 32 * f + 32]]
            whole = jnp.concatenate(pieces, axis=0)
            for t in range(WIDE // 128):
                lanes = slice(128 * t, 128 * t + 128)
                base = ROWS * (f * ELEM + 128 * t) + ROWS * WIDE * h
                for c in range(ROWS):
                    chunk = whole[128 * c : min(128 * c + 128, TRACE), lanes]
                    if c == ROWS - 1:
                        chunk = jnp.concatenate([chunk, jnp.zeros((128 - chunk.shape[0], 128), f32)], axis=0)
                    turned = chunk.T
                    mine[pl.ds(base + c, 128, stride=ROWS), :] = turned
                    pool[pl.ds(base + c, 128, stride=ROWS), :] = turned
        return carry

    lax.fori_loop(0, ELEM // WIDE, predict, 0)

    if remote:
        pl.semaphore_wait(barrier, greeted)

    copies = []
    for at, (axis, step, there, target, first, land, rows) in enumerate(links):
        ref = (exs_ref, exd_ref, exz_ref)[at // 2]
        side = at % 2

        def export(t, carry, ref=ref, side=side, first=first):
            for u in range(16):
                slot = ref[side, t * 16 + u]
                ship[pl.ds(ROWS * (first + t * 16 + u), ROWS), :] = mine[pl.ds(ROWS * slot, ROWS), :]
            return carry

        lax.fori_loop(0, rows // 16, export, 0)
        source = ship.at[pl.ds(ROWS * first, ROWS * rows), :]
        goal = pool.at[pl.ds(ROWS * (4 * ELEM + land), ROWS * rows), :]
        if remote:
            other = at ^ 1
            copy = pltpu.make_async_remote_copy(
                src_ref=source,
                dst_ref=goal,
                send_sem=send_sem.at[at],
                recv_sem=recv_sem.at[other],
                device_id={axis: target},
                device_id_type=MESH,
            )
            pl.when(there)(copy.start)
        else:
            copy = pltpu.make_async_copy(source, goal, send_sem.at[at])
            copy.start()
        copies.append(copy)

    stiff_weights(vol_ref, 1.0, w_vol_h, w_vol_l)
    for o in range(3):
        w_rot[80 * o : 80 * o + 80] = stacked(rot_ref[o], FACE)
        w_rot3[80 * o : 80 * o + 80] = packed_rotate(rot_ref[o])
    for f in range(4):
        w_lift[f] = stacked(-lift_ref[f], FACE)

    def volume(h, carry):
        cs = columns(h)
        slabs = transport(lambda b: integral[b, :, cs], geometry(h), w_jac, w_vol_h, w_vol_l, mix)
        for s in range(4):
            total[s, :, cs] = slabs[s]
        return carry

    lax.fori_loop(0, ELEM // WIDE, volume, 0)
    cols_copy.wait()

    for at, (axis, step, there, target, first, land, rows) in enumerate(links):
        copy = copies[at]
        if remote:
            arrived = pltpu.make_async_remote_copy(
                src_ref=ship.at[pl.ds(ROWS * first, ROWS * rows), :],
                dst_ref=pool.at[pl.ds(ROWS * (4 * ELEM + first), ROWS * rows), :],
                send_sem=send_sem.at[at],
                recv_sem=recv_sem.at[at],
                device_id={axis: target},
                device_id_type=MESH,
            )

            @pl.when(there)
            def _(copy=copy, arrived=arrived):
                copy.wait_send()
                arrived.wait_recv()
        else:
            copy.wait()

    def faces(step, carry):
        f, h = step // 2, step % 2
        cs = columns(h)

        def fetch(t, inner):
            for u in range(16):
                at = cols_s[f, h * WIDE + t * 16 + u]
                near[pl.ds(t * 16 + u, ROWS, stride=WIDE), :] = pool[pl.ds(at, ROWS), :]
            return inner

        lax.fori_loop(0, WIDE // 16, fetch, 0)
        halves = []
        for t in range(WIDE // 128):
            turned = [near[WIDE * c + 128 * t : WIDE * c + 128 * t + 128, :].T for c in range(ROWS)]
            halves.append(jnp.concatenate([turned[0], turned[1], turned[2][: TRACE - 256]], axis=0))
        high, low = split(jnp.concatenate(halves, axis=1))
        turn = jnp.broadcast_to(orient_ref[pl.ds(f, 1), cs], (8, WIDE))[None]
        nb = []
        for s in range(4):
            rows = slice(80 * s, min(80 * s + 80, TRACE))
            operand = jnp.concatenate([high[rows], low[rows], high[rows]], axis=0)
            turned = dot(w_rot[...] if s < 3 else w_rot3[...], operand).reshape(3, FACE, 8, WIDE)
            nb.append(jnp.where(turn == 0, turned[0], jnp.where(turn == 1, turned[1], turned[2])))
        normal = [
            0.5 * jnp.broadcast_to(nrm_ref[f, j : j + 1, cs], (8, WIDE))[None] for j in range(3)
        ]
        speed = 0.5 * jnp.broadcast_to(speed_ref[:, cs], (8, WIDE))[None]
        flux = []
        for i in range(FACE):
            there = jnp.stack([nb[s][i] for s in range(4)])
            here = own[f, i, :, cs].reshape(4, 8, WIDE)
            high, low = split((here + there).reshape(32, WIDE))
            moved = dot(w_jac[...], jnp.concatenate([high, low, high], axis=0))
            value = speed * (here - there)
            for j in range(3):
                value = value + normal[j] * moved[32 * j : 32 * j + 32].reshape(4, 8, WIDE)
            flux.append(value)
        for s in range(4):
            high, low = split(jnp.concatenate([flux[i][s] for i in range(FACE)], axis=0))
            operand = jnp.concatenate([high, low, high], axis=0)
            total[s, :, cs] += dot(w_lift[f], operand)
        return carry

    lax.fori_loop(0, 8, faces, 0)

    for h in range(ELEM // WIDE):
        cs = slice(h * WIDE, h * WIDE + WIDE)
        fine = jnp.broadcast_to(cluster_ref[:, cs], (8, WIDE)) == 0
        for b in range(BASIS):
            for s in range(4):
                n = min(8, QUANT - 8 * s)
                update = jnp.where(fine, total[s, 8 * b : 8 * b + 8, cs], 0.0)[:n]
                out_ref[b, 8 * s : 8 * s + n, cs] = state_ref[b, 8 * s : 8 * s + n, cs] + update


def update_call(remote, *args):
    vmem = pl.BlockSpec(memory_space=pltpu.VMEM)
    smem = pl.BlockSpec(memory_space=pltpu.SMEM)
    return pl.pallas_call(
        functools.partial(kernel, remote),
        out_shape=jax.ShapeDtypeStruct((BASIS, QUANT, ELEM), f32),
        in_specs=[vmem] * 8 + [smem] * 3 + [vmem] * 6,
        out_specs=vmem,
        scratch_shapes=[
            pltpu.VMEM((BASIS, 32, ELEM), f32),
            pltpu.VMEM((BASIS, 32, ELEM), f32),
            pltpu.VMEM((4, 480, WIDE), f32),
            pltpu.VMEM((4, FACE, 32, ELEM), f32),
            pltpu.VMEM((4, 160, ELEM), f32),
            pltpu.VMEM((ROWS * 4 * ELEM, 128), f32),
            pltpu.VMEM((ROWS * 6 * ELEM, 128), f32),
            pltpu.VMEM((ROWS * 2 * ELEM, 128), f32),
            pltpu.VMEM((ROWS * WIDE, 128), f32),
            pltpu.VMEM((4, ELEM), i32),
            pltpu.SMEM((4, ELEM), i32),
            pltpu.VMEM((128, 128), f32),
            pltpu.VMEM((96, 96), bf16),
            pltpu.VMEM((160, 480), bf16),
            pltpu.VMEM((160, 480), bf16),
            pltpu.VMEM((160, 480), bf16),
            pltpu.VMEM((160, 480), bf16),
            pltpu.VMEM((320, 480), bf16),
            pltpu.VMEM((128, 480), bf16),
            pltpu.VMEM((240, 240), bf16),
            pltpu.VMEM((240, 96), bf16),
            pltpu.VMEM((4, 160, 240), bf16),
            pltpu.SemaphoreType.DMA,
            pltpu.SemaphoreType.DMA((6,)),
            pltpu.SemaphoreType.DMA((6,)),
        ],
        compiler_params=pltpu.CompilerParams(
            vmem_limit_bytes=56 * 2**20,
            **(dict(collective_id=0, has_side_effects=True) if remote else {}),
        ),
    )(*args)


def per_device(state, geometry, normals, wave_speed, cluster, *rest):
    return update_call(
        True, state, geometry, normals, wave_speed.reshape(1, ELEM), cluster.reshape(1, ELEM), *rest
    )


def solution(mesh):
    whole = ("strike", "dip", "depth")
    placed = (
        (P(None, None, whole),) * 3 + (P(whole),) * 2 + (P(None, whole),) * 6 + (P(),) * 6
    )
    return jax.shard_map(
        per_device,
        mesh=mesh,
        in_specs=placed,
        out_specs=P(None, None, whole),
        check_vma=False,
    )
```

profile of v0, /device:TPU:109, one launch (start us, length us, event | category | flops | bytes accessed | tf_op | source)
XLA Modules:
  0.0 44.6 jit_solution(10904055736897566073)
XLA Ops:
  0.0 1.3 %copy.21.rot_ref = f32[3,10,10]{2,1,0:T(8,128)} copy(f32[3,10,10]{2,0,1:T(4,128)} %param.33) | data formatting | bytes 2400 | tf_op args[16]
  1.3 1.3 %copy.18.nrm_ref = f32[4,3,512]{2,1,0:T(4,128)} copy(f32[4,3,512]{2,0,1:T(4,128)} %param.19) | data formatting | bytes 49152 | tf_op args[2]
  2.7 1.3 %copy.19.proj_ref = f32[4,10,20]{2,1,0:T(8,128)} copy(f32[4,10,20]{2,0,1:T(4,128)} %param.31) | data formatting | bytes 6400 | tf_op args[14]
  4.0 1.4 %copy.20.lift_ref = f32[4,20,10]{2,1,0:T(8,128)} copy(f32[4,20,10]{1,0,2:T(4,128)} %param.32) | data formatting | bytes 6400 | tf_op args[15]
  5.5 36.6 %shard_map.163 = f32[20,27,512]{2,1,0:T(8,128)} custom-call(f32[20,27,512]{2,1,0:T(8,128)} %state_ref.1, f32[3,3,512]{2,1,0:T(4,128)} %geo_ref.1, f32[4,3,512]{2,1,0:T(4,128)} %copy.18.nrm_ref, f32[1,512]{1,0:T(1,128)} %bitcast.2, s32[1,512]{1,0:T(1,128)} %bitcast.3, s32[4,512]{1,0:T(4,128)} %nbi_ref.1, s32[4,512]{1,0:T(4,128)} %nbf_ref.1, ...), custom_call_target="tpu_custom_call" | custom-call | tf_op jit(solution)/shard_map/pallas_call | solution.py:419
  42.1 2.5 %copy.23 = f32[20,27,512]{2,1,0:T(8,128)} copy(f32[20,27,512]{2,1,0:T(8,128)} %shard_map.163) | data formatting | bytes 2211840
where the time goes:
time: 44.9 us; the launch traced here: 44.6 us
  Pallas kernels  36.6 us (82%)
  local copies, waits for them, and re-layouts  7.97 us (18%)
    pallas_call x1, Pallas kernels, update_call(): pl.pallas_call(functools.partial(kernel, remote), out_shape=jax.ShapeDtyp...  36.6 us
    unnamed x5, local copies, waits for them, and re-layouts  7.97 us

commit v1 on v0

v1 whole, which is shorter than its diff:
```python
import functools
import math

import jax
import jax.numpy as jnp
from jax import lax
from jax.experimental import pallas as pl
from jax.experimental.pallas import tpu as pltpu
from jax.sharding import PartitionSpec as P

MESH = pl.DeviceIdType.MESH
BASIS, QUANT, FACE = 20, 27, 10
ELEM = 512
TIME_STEP = 0.5
ORDER = 4
WIDE = 256
ROWS = 3
TRACE = 272
f32, bf16, i32 = jnp.float32, jnp.bfloat16, jnp.int32

LINKS = (
    ("strike", 0, 256),
    ("strike", 256, 256),
    ("dip", 512, 128),
    ("dip", 640, 128),
    ("depth", 768, 128),
    ("depth", 896, 128),
)


def dot(a, b):
    return jnp.dot(a, b, preferred_element_type=f32)


def split(x):
    high = x.astype(bf16)
    return high, (x - high.astype(f32)).astype(bf16)


def rep8(m):
    n, k = m.shape
    return jnp.broadcast_to(m[:, None, :], (n, 8, k)).reshape(n * 8, k)


def iota(shape, dim):
    return lax.broadcasted_iota(i32, shape, dim)


def spread(m, parts, count, chosen):
    n, k = m.shape
    width = parts * count * 8
    col = iota((k, width), 1)
    row = iota((k, width), 0)
    put = jnp.zeros((k, width), jnp.bool_)
    for part in chosen:
        put = put | ((col - part * count * 8) >> 3 == row)
    wide = dot(rep8(m.astype(f32)).astype(bf16), jnp.where(put, 1.0, 0.0).astype(bf16))
    same = (iota((n * 8, width), 0) & 7) == (iota((n * 8, width), 1) & 7)
    return jnp.where(same, wide, 0.0)


def stacked(m, count):
    high, low = split(m)
    return (spread(high, 3, count, (0, 1)) + spread(low, 3, count, (2,))).astype(bf16)


def jacobian_weights(jac_ref, tmp_ref, out_ref):
    tmp_ref[...] = jnp.zeros((128, 128), f32)
    for j in range(3):
        high, low = split(jac_ref[j])
        at = slice(32 * j, 32 * j + QUANT)
        tmp_ref[0:QUANT, at] = high.astype(f32)
        tmp_ref[32 : 32 + QUANT, at] = high.astype(f32)
        tmp_ref[64 : 64 + QUANT, at] = low.astype(f32)
    out_ref[...] = tmp_ref[...].T[:96, :96].astype(bf16)


def stiff_weights(mat_ref, sign, high_ref, low_ref):
    high_sum = jnp.zeros((160, 960), f32)
    low_sum = jnp.zeros((160, 480), f32)
    for d in range(3):
        high, low = split(sign * mat_ref[d])
        high_sum = high_sum + spread(high, 6, BASIS, (d, d + 3))
        low_sum = low_sum + spread(low, 3, BASIS, (d,))
    high_ref[...] = high_sum.astype(bf16)
    low_ref[...] = low_sum.astype(bf16)


def packed_project(m):
    high, low = split(m)
    row = iota((32, FACE), 0)
    third = (row * 171) >> 9
    pick = jnp.where(third == iota((32, FACE), 1), 1.0, 0.0).astype(bf16)
    total = jnp.zeros((32, 480), f32)
    for part_from, part_to, piece in ((0, 1, high), (2, 2, low)):
        rows = dot(pick, piece).astype(bf16)
        col = iota((BASIS, 480), 1)
        put = jnp.zeros((BASIS, 480), jnp.bool_)
        for part in range(part_from, part_to + 1):
            put = put | ((col - part * 160) >> 3 == iota((BASIS, 480), 0))
        total = total + dot(rows, jnp.where(put, 1.0, 0.0).astype(bf16))
    out_row = iota((32, 480), 0)
    same = (out_row - 3 * ((out_row * 171) >> 9)) == (iota((32, 480), 1) & 7)
    return jnp.where(same & (out_row < 30), total, 0.0).astype(bf16)


def packed_rotate(m):
    high, low = split(m)
    total = jnp.zeros((80, 96), f32)
    col = iota((FACE, 96), 1)
    for part_from, part_to, piece in ((0, 1, high), (2, 2, low)):
        put = jnp.zeros((FACE, 96), jnp.bool_)
        for part in range(part_from, part_to + 1):
            inner = col - part * 32
            put = put | ((inner >= 0) & (inner < 30) & ((inner * 171) >> 9 == iota((FACE, 96), 0)))
        total = total + dot(rep8(piece.astype(f32)).astype(bf16), jnp.where(put, 1.0, 0.0).astype(bf16))
    inner = iota((80, 96), 1) & 31
    same = (inner - 3 * ((inner * 171) >> 9)) == (iota((80, 96), 0) & 7)
    return jnp.where(same, total, 0.0).astype(bf16)


def mixed(field, geo, weights):
    high, low = split(field)
    moved = dot(weights, jnp.concatenate([high, low, high], axis=0))
    n = field.shape[1]
    parts = [moved[32 * j : 32 * j + 32].reshape(4, 8, n) for j in range(3)]
    return [
        (geo[d][0] * parts[0] + geo[d][1] * parts[1] + geo[d][2] * parts[2]).reshape(32, n)
        for d in range(3)
    ]


def mix_steps(load, geo, jac_ref, mix_ref):
    def step(b):
        first, second = (mixed(load(b + i), geo, jac_ref[...]) for i in range(2))
        for d in range(3):
            for s in range(4):
                rows = slice(8 * s, 8 * s + 8)
                high, low = split(jnp.concatenate([first[d][rows], second[d][rows]], axis=0))
                at = (d * BASIS + b) * 8
                mix_ref[s, at : at + 16, :] = high
                mix_ref[s, 480 + at : 480 + at + 16, :] = low

    return [functools.partial(step, b) for b in range(0, BASIS, 2)]


def stiff_steps(mix_ref, weights_ref, low_ref, store):
    def step(s):
        store(s, dot(weights_ref[...], mix_ref[s]) + dot(low_ref[...], mix_ref[s, :480]))

    return [functools.partial(step, s) for s in range(4)]


def run(*phases):
    for phase in phases:
        for step in phase:
            step()


def kernel(
    remote,
    state_ref,
    geo_ref,
    nrm_ref,
    speed_ref,
    cluster_ref,
    nbi_ref,
    nbf_ref,
    orient_ref,
    exs_ref,
    exd_ref,
    exz_ref,
    stiff_ref,
    vol_ref,
    jac_ref,
    proj_ref,
    lift_ref,
    rot_ref,
    out_ref,
    field_a,
    field_b,
    integral_a,
    integral_b,
    mix_a,
    mix_b,
    times,
    own,
    total,
    mine,
    pool,
    ship,
    near,
    cols_v,
    cols_s,
    exp_v,
    exp_s,
    tmp,
    tmp2,
    w_jac,
    w_stiff_h,
    w_stiff_l,
    w_vol_h,
    w_vol_l,
    w_proj,
    w_proj3,
    w_rot,
    w_rot3,
    w_lift,
    cols_sem,
    send_sem,
    recv_sem,
):
    fields, integrals, mixes = (field_a, field_b), (integral_a, integral_b), (mix_a, mix_b)
    halves = range(ELEM // WIDE)

    links = []
    for at, (axis, first, rows) in enumerate(LINKS):
        step = -1 if at % 2 == 0 else 1
        if remote:
            pos, count = lax.axis_index(axis), lax.axis_size(axis)
            there = pos > 0 if step < 0 else pos < count - 1
            target = jnp.clip(pos + step, 0, count - 1)
        else:
            there, target = True, None
        land = first + rows if step < 0 else first - rows
        links.append((axis, there, target, first, land, rows))

    if remote:
        barrier = pltpu.get_barrier_semaphore()
        greeted = 0
        for axis, there, target, *_ in links:

            @pl.when(there)
            def _(axis=axis, target=target):
                pl.semaphore_signal(barrier, inc=1, device_id={axis: target}, device_id_type=MESH)

            greeted = greeted + there.astype(i32)

    index = nbi_ref[...]
    cols_v[...] = ROWS * jnp.where(index < ELEM, nbf_ref[...] * ELEM + index, 3 * ELEM + index)
    exp_v[:, 0:256] = ROWS * exs_ref[...]
    exp_v[:, 256:384] = ROWS * exd_ref[...]
    exp_v[:, 384:512] = ROWS * exz_ref[...]
    index_copies = [
        pltpu.make_async_copy(cols_v, cols_s, cols_sem.at[0]),
        pltpu.make_async_copy(exp_v, exp_s, cols_sem.at[1]),
    ]
    for copy in index_copies:
        copy.start()

    jacobian_weights(jac_ref, tmp, w_jac)
    stiff_weights(stiff_ref, -1.0, w_stiff_h, w_stiff_l)
    for f in range(4):
        w_proj[80 * f : 80 * f + 80] = stacked(proj_ref[:, f, :], BASIS)
        w_proj3[32 * f : 32 * f + 32] = packed_project(proj_ref[:, f, :])

    zeros5 = jnp.zeros((5, WIDE), f32)

    def columns(h):
        return slice(h * WIDE, h * WIDE + WIDE)

    def geometry(h):
        return [
            [jnp.broadcast_to(geo_ref[d, j : j + 1, columns(h)], (8, WIDE))[None] for j in range(3)]
            for d in range(3)
        ]

    fine = cluster_ref[...] == 0
    for degree in range(ORDER):
        base = TIME_STEP ** (degree + 1) / math.factorial(degree + 1)
        coarse = base * (2.0 ** (degree + 1) - 1.0)
        times[degree] = jnp.broadcast_to(jnp.where(fine, f32(base), f32(coarse)), (8, ELEM))

    for h in halves:
        for b in range(BASIS):
            value = jnp.concatenate([state_ref[b, :, columns(h)], zeros5], axis=0)
            fields[h][b] = value
            integrals[h][b] = (times[0, :, columns(h)][None] * value.reshape(4, 8, WIDE)).reshape(32, WIDE)

    def predict(degree, carry):
        phases = [mix_steps(lambda b, h=h: fields[h][b], geometry(h), w_jac, mixes[h]) for h in halves]
        for h in halves:

            def store(s, value, h=h):
                value = value.reshape(BASIS, 8, WIDE)
                rows = slice(8 * s, 8 * s + 8)
                fields[h][:, rows, :] = value
                integrals[h][:, rows, :] += times[degree, :, columns(h)][None] * value

            phases.append(stiff_steps(mixes[h], w_stiff_h, w_stiff_l, store))
        run(*phases)
        return carry

    lax.fori_loop(1, ORDER, predict, 0)

    for h in halves:
        for s in range(4):
            high, low = split(integrals[h][:, 8 * s : 8 * s + 8, :].reshape(BASIS * 8, WIDE))
            operand = jnp.concatenate([high, low, high], axis=0)
            traces = dot(w_proj[...], operand)
            for f in range(4):
                own[f, :, 8 * s : 8 * s + 8, columns(h)] = traces[80 * f : 80 * f + 80].reshape(FACE, 8, WIDE)
            if s == 3:
                packed = dot(w_proj3[...], operand)
        for f in range(4):
            pieces = [own[f, :, 8 * s : 8 * s + 8, columns(h)].reshape(80, WIDE) for s in range(3)]
            whole = jnp.concatenate(pieces + [packed[32 * f : 32 * f + 32]], axis=0)
            for t in range(WIDE // 128):
                base = ROWS * (f * ELEM + h * WIDE + 128 * t)
                for c in range(ROWS):
                    chunk = whole[128 * c : min(128 * c + 128, TRACE), 128 * t : 128 * t + 128]
                    if c == ROWS - 1:
                        chunk = jnp.concatenate([chunk, jnp.zeros((128 - chunk.shape[0], 128), f32)], axis=0)
                    turned = chunk.T
                    mine[pl.ds(base + c, 128, stride=ROWS), :] = turned
                    pool[pl.ds(base + c, 128, stride=ROWS), :] = turned

    for copy in index_copies:
        copy.wait()
    if remote:
        pl.semaphore_wait(barrier, greeted)

    copies = []
    for at, (axis, there, target, first, land, rows) in enumerate(links):
        side = at % 2
        lane = (0, 256, 384)[at // 2]

        def export(t, carry, side=side, first=first, lane=lane):
            for u in range(64):
                row = exp_s[side, lane + t * 64 + u]
                ship[pl.ds(ROWS * (first + t * 64 + u), ROWS), :] = mine[pl.ds(row, ROWS), :]
            return carry

        lax.fori_loop(0, rows // 64, export, 0)
        source = ship.at[pl.ds(ROWS * first, ROWS * rows), :]
        goal = pool.at[pl.ds(ROWS * (4 * ELEM + land), ROWS * rows), :]
        if remote:
            copy = pltpu.make_async_remote_copy(
                src_ref=source,
                dst_ref=goal,
                send_sem=send_sem.at[at],
                recv_sem=recv_sem.at[at ^ 1],
                device_id={axis: target},
                device_id_type=MESH,
            )
            pl.when(there)(copy.start)
        else:
            copy = pltpu.make_async_copy(source, goal, send_sem.at[at])
            copy.start()
        copies.append(copy)

    stiff_weights(vol_ref, 1.0, w_vol_h, w_vol_l)
    tmp2[...] = jnp.zeros((128, 128), f32)
    for f in range(4):
        tmp2[16 * f : 16 * f + FACE, 0:BASIS] = lift_ref[:, f, :]
    lifts = tmp2[...].T
    for o in range(3):
        w_rot[80 * o : 80 * o + 80] = stacked(rot_ref[:, o, :], FACE)
        w_rot3[80 * o : 80 * o + 80] = packed_rotate(rot_ref[:, o, :])
    for f in range(4):
        w_lift[f] = stacked(-lifts[0:BASIS, 16 * f : 16 * f + FACE], FACE)

    phases = [mix_steps(lambda b, h=h: integrals[h][b], geometry(h), w_jac, mixes[h]) for h in halves]
    for h in halves:

        def store(s, value, h=h):
            total[s, :, columns(h)] = value

        phases.append(stiff_steps(mixes[h], w_vol_h, w_vol_l, store))
    run(*phases)

    for at, (axis, there, target, first, land, rows) in enumerate(links):
        copy = copies[at]
        if remote:
            arrived = pltpu.make_async_remote_copy(
                src_ref=ship.at[pl.ds(ROWS * first, ROWS * rows), :],
                dst_ref=pool.at[pl.ds(ROWS * (4 * ELEM + first), ROWS * rows), :],
                send_sem=send_sem.at[at],
                recv_sem=recv_sem.at[at],
                device_id={axis: target},
                device_id_type=MESH,
            )

            @pl.when(there)
            def _(copy=copy, arrived=arrived):
                copy.wait_send()
                arrived.wait_recv()
        else:
            copy.wait()

    def fetch(f, first, count):
        for n in range(first, first + count):
            near[pl.ds(ROWS * n, ROWS), :] = pool[pl.ds(cols_s[f, n], ROWS), :]

    def turned(f, h):
        tiles = []
        for t in range(WIDE // 128):
            base = ROWS * (h * WIDE + 128 * t)
            parts = [near[pl.ds(base + c, 128, stride=ROWS), :].T for c in range(ROWS)]
            tiles.append(jnp.concatenate([parts[0], parts[1], parts[2][: TRACE - 256]], axis=0))
        high, low = split(jnp.concatenate(tiles, axis=1))
        turn = jnp.broadcast_to(orient_ref[pl.ds(f, 1), columns(h)], (8, WIDE))[None]
        slabs = []
        for s in range(4):
            rows = slice(80 * s, min(80 * s + 80, TRACE))
            operand = jnp.concatenate([high[rows], low[rows], high[rows]], axis=0)
            ways = dot(w_rot[...] if s < 3 else w_rot3[...], operand).reshape(3, FACE, 8, WIDE)
            slabs.append(jnp.where(turn == 0, ways[0], jnp.where(turn == 1, ways[1], ways[2])))
        return slabs

    def fluxes(f, h, slabs):
        normal = [
            0.5 * jnp.broadcast_to(nrm_ref[j, pl.ds(f, 1), columns(h)], (8, WIDE))[None] for j in range(3)
        ]
        speed = 0.5 * jnp.broadcast_to(speed_ref[:, columns(h)], (8, WIDE))[None]
        flux = []
        for i in range(FACE):
            there = jnp.stack([slabs[s][i] for s in range(4)])
            here = own[f, i, :, columns(h)].reshape(4, 8, WIDE)
            high, low = split((here + there).reshape(32, WIDE))
            moved = dot(w_jac[...], jnp.concatenate([high, low, high], axis=0))
            value = speed * (here - there)
            for j in range(3):
                value = value + normal[j] * moved[32 * j : 32 * j + 32].reshape(4, 8, WIDE)
            flux.append(value)
        return flux

    def lifted(f, h, flux):
        for s in range(4):
            high, low = split(jnp.concatenate([flux[i][s] for i in range(FACE)], axis=0))
            operand = jnp.concatenate([high, low, high], axis=0)
            total[s, :, columns(h)] += dot(w_lift[f], operand)

    fetch(0, 0, ELEM)

    def faces(f, carry):
        later = jnp.minimum(f + 1, 3)
        slabs = [turned(f, h) for h in halves]
        flux = []
        for h in halves:
            flux.append(fluxes(f, h, slabs[h]))
            fetch(later, h * (ELEM // 4), ELEM // 4)
        for h in halves:
            lifted(f, h, flux[h])
            fetch(later, ELEM // 2 + h * (ELEM // 4), ELEM // 4)
        return carry

    lax.fori_loop(0, 4, faces, 0)

    for h in halves:
        keep = jnp.broadcast_to(cluster_ref[:, columns(h)], (8, WIDE)) == 0
        for b in range(BASIS):
            for s in range(4):
                n = min(8, QUANT - 8 * s)
                update = jnp.where(keep, total[s, 8 * b : 8 * b + 8, columns(h)], 0.0)[:n]
                out_ref[b, 8 * s : 8 * s + n, columns(h)] = (
                    state_ref[b, 8 * s : 8 * s + n, columns(h)] + update
                )


def update_call(remote, *args):
    vmem = pl.BlockSpec(memory_space=pltpu.VMEM)
    return pl.pallas_call(
        functools.partial(kernel, remote),
        out_shape=pltpu.VMEM((BASIS, QUANT, ELEM), f32),
        in_specs=[vmem] * 17,
        out_specs=vmem,
        scratch_shapes=[
            pltpu.VMEM((BASIS, 32, WIDE), f32),
            pltpu.VMEM((BASIS, 32, WIDE), f32),
            pltpu.VMEM((BASIS, 32, WIDE), f32),
            pltpu.VMEM((BASIS, 32, WIDE), f32),
            pltpu.VMEM((4, 960, WIDE), bf16),
            pltpu.VMEM((4, 960, WIDE), bf16),
            pltpu.VMEM((ORDER, 8, ELEM), f32),
            pltpu.VMEM((4, FACE, 32, ELEM), f32),
            pltpu.VMEM((4, 160, ELEM), f32),
            pltpu.VMEM((ROWS * 4 * ELEM, 128), f32),
            pltpu.VMEM((ROWS * 6 * ELEM, 128), f32),
            pltpu.VMEM((ROWS * 2 * ELEM, 128), f32),
            pltpu.VMEM((ROWS * ELEM, 128), f32),
            pltpu.VMEM((4, ELEM), i32),
            pltpu.SMEM((4, ELEM), i32),
            pltpu.VMEM((2, ELEM), i32),
            pltpu.SMEM((2, ELEM), i32),
            pltpu.VMEM((128, 128), f32),
            pltpu.VMEM((128, 128), f32),
            pltpu.VMEM((96, 96), bf16),
            pltpu.VMEM((160, 960), bf16),
            pltpu.VMEM((160, 480), bf16),
            pltpu.VMEM((160, 960), bf16),
            pltpu.VMEM((160, 480), bf16),
            pltpu.VMEM((320, 480), bf16),
            pltpu.VMEM((128, 480), bf16),
            pltpu.VMEM((240, 240), bf16),
            pltpu.VMEM((240, 96), bf16),
            pltpu.VMEM((4, 160, 240), bf16),
            pltpu.SemaphoreType.DMA((2,)),
            pltpu.SemaphoreType.DMA((6,)),
            pltpu.SemaphoreType.DMA((6,)),
        ],
        compiler_params=pltpu.CompilerParams(
            vmem_limit_bytes=56 * 2**20,
            **(dict(collective_id=0, has_side_effects=True) if remote else {}),
        ),
    )(*args)


def arranged(args):
    state, geometry, normals, speed, cluster, *rest, proj, lift, rot = args
    return (
        state,
        geometry,
        jnp.transpose(normals, (1, 0, 2)),
        speed.reshape(1, ELEM),
        cluster.reshape(1, ELEM),
        *rest,
        jnp.transpose(proj, (1, 0, 2)),
        jnp.transpose(lift, (2, 0, 1)),
        jnp.transpose(rot, (1, 0, 2)),
    )


def per_device(*args):
    return update_call(True, *arranged(args))


def solution(mesh):
    whole = ("strike", "dip", "depth")
    placed = (
        (P(None, None, whole),) * 3 + (P(whole),) * 2 + (P(None, whole),) * 6 + (P(),) * 6
    )
    return jax.shard_map(
        per_device,
        mesh=mesh,
        in_specs=placed,
        out_specs=P(None, None, whole),
        check_vma=False,
    )
```

time: 44.9 us -> 29.1 us (0.65)
  Pallas kernels: 36.6 us -> 27.9 us
  local copies, waits for them, and re-layouts: 7.97 us -> 1.06 us
    pallas_call x1, Pallas kernels: 36.6 us -> 27.9 us  [update_call(): pl.pallas_call(functools.partial(kernel, remote), out_shape=pltpu.VMEM((B...]
    unnamed x5 -> x1, local copies, waits for them, and re-layouts: 7.97 us -> 1.06 us
where the time goes in v1:
time: 29.1 us; the launch traced here: 29 us
  Pallas kernels  27.9 us (96%)
  local copies, waits for them, and re-layouts  1.06 us (4%)
    pallas_call x1, Pallas kernels, update_call(): pl.pallas_call(functools.partial(kernel, remote), out_shape=pltpu.VMEM((B...  27.9 us
    unnamed x1, local copies, waits for them, and re-layouts  1.06 us

profile of v1, /device:TPU:109, one launch (start us, length us, event | category | flops | bytes accessed | tf_op | source)
XLA Modules:
  0.0 29.0 jit_solution(18006767847186325097)
XLA Ops:
  0.0 27.9 %shard_map.163 = f32[20,27,512]{2,1,0:T(8,128)S(1)} custom-call(f32[20,27,512]{2,1,0:T(8,128)} %state_ref.1, f32[3,3,512]{2,1,0:T(4,128)} %geo_ref.1, f32[3,4,512]{2,1,0:T(4,128)} %bitcast.6, f32[1,512]{1,0:T(1,128)} %bitcast.10, s32[1,512]{1,0:T(1,128)} %bitcast.11, s32[4,512]{1,0:T(4,128)} %nbi_ref.1, s32[4,512]{1,0:T(4,128)} %nbf_ref.1, ...), custom_call_target="tpu_custom_call" | custom-call | tf_op jit(solution)/shard_map/pallas_call | solution.py:463
  27.9 1.1 %copy.19 = f32[20,27,512]{2,1,0:T(8,128)} copy(f32[20,27,512]{2,1,0:T(8,128)S(1)} %shard_map.163) | data formatting | bytes 2211840

commit v2 on v1

--- a/solution.py
+++ b/solution.py
@@ -46,26 +46,40 @@
     return lax.broadcasted_iota(i32, shape, dim)
 
 
-def spread(m, parts, count, chosen):
+def ones_where(mask):
+    return jnp.where(mask, 1.0, 0.0).astype(bf16)
+
+
+def expander(count):
+    shape = (96, 24 * count)
+    row, entry = iota(shape, 0), iota(shape, 1) >> 3
+    part = row >> 5
+    inner = row & 31
+    return ones_where((inner < count) & (entry == part * count + inner))
+
+
+def diagonal(width):
+    return (iota((8, width), 0) == (iota((8, width), 1) & 7))[None]
+
+
+def kron8(rows, expand, diag):
+    n, width = rows.shape[0], expand.shape[1]
+    wide = dot(rep8(rows).astype(bf16), expand).reshape(n, 8, width)
+    return jnp.where(diag, wide, 0.0).reshape(n * 8, width).astype(bf16)
+
+
+def lay(tmp_ref, at, m):
     n, k = m.shape
-    width = parts * count * 8
-    col = iota((k, width), 1)
-    row = iota((k, width), 0)
-    put = jnp.zeros((k, width), jnp.bool_)
-    for part in chosen:
-        put = put | ((col - part * count * 8) >> 3 == row)
-    wide = dot(rep8(m.astype(f32)).astype(bf16), jnp.where(put, 1.0, 0.0).astype(bf16))
-    same = (iota((n * 8, width), 0) & 7) == (iota((n * 8, width), 1) & 7)
-    return jnp.where(same, wide, 0.0)
-
-
-def stacked(m, count):
-    high, low = split(m)
-    return (spread(high, 3, count, (0, 1)) + spread(low, 3, count, (2,))).astype(bf16)
+    high, low = (piece.astype(f32) for piece in split(m))
+    for part, piece in enumerate((high, high, low)):
+        tmp_ref[at : at + n, 32 * part : 32 * part + k] = piece
+
+
+def third(x):
+    return (x * 171) >> 9
 
 
 def jacobian_weights(jac_ref, tmp_ref, out_ref):
-    tmp_ref[...] = jnp.zeros((128, 128), f32)
     for j in range(3):
         high, low = split(jac_ref[j])
         at = slice(32 * j, 32 * j + QUANT)
@@ -75,48 +89,52 @@
     out_ref[...] = tmp_ref[...].T[:96, :96].astype(bf16)
 
 
-def stiff_weights(mat_ref, sign, high_ref, low_ref):
-    high_sum = jnp.zeros((160, 960), f32)
-    low_sum = jnp.zeros((160, 480), f32)
+def stiff_weights(mat_ref, sign, tmp_ref, expand, diag, high_ref, low_ref):
     for d in range(3):
         high, low = split(sign * mat_ref[d])
-        high_sum = high_sum + spread(high, 6, BASIS, (d, d + 3))
-        low_sum = low_sum + spread(low, 3, BASIS, (d,))
-    high_ref[...] = high_sum.astype(bf16)
-    low_ref[...] = low_sum.astype(bf16)
-
-
-def packed_project(m):
-    high, low = split(m)
-    row = iota((32, FACE), 0)
-    third = (row * 171) >> 9
-    pick = jnp.where(third == iota((32, FACE), 1), 1.0, 0.0).astype(bf16)
-    total = jnp.zeros((32, 480), f32)
-    for part_from, part_to, piece in ((0, 1, high), (2, 2, low)):
-        rows = dot(pick, piece).astype(bf16)
-        col = iota((BASIS, 480), 1)
-        put = jnp.zeros((BASIS, 480), jnp.bool_)
-        for part in range(part_from, part_to + 1):
-            put = put | ((col - part * 160) >> 3 == iota((BASIS, 480), 0))
-        total = total + dot(rows, jnp.where(put, 1.0, 0.0).astype(bf16))
-    out_row = iota((32, 480), 0)
-    same = (out_row - 3 * ((out_row * 171) >> 9)) == (iota((32, 480), 1) & 7)
-    return jnp.where(same & (out_row < 30), total, 0.0).astype(bf16)
-
-
-def packed_rotate(m):
-    high, low = split(m)
-    total = jnp.zeros((80, 96), f32)
-    col = iota((FACE, 96), 1)
-    for part_from, part_to, piece in ((0, 1, high), (2, 2, low)):
-        put = jnp.zeros((FACE, 96), jnp.bool_)
-        for part in range(part_from, part_to + 1):
-            inner = col - part * 32
-            put = put | ((inner >= 0) & (inner < 30) & ((inner * 171) >> 9 == iota((FACE, 96), 0)))
-        total = total + dot(rep8(piece.astype(f32)).astype(bf16), jnp.where(put, 1.0, 0.0).astype(bf16))
-    inner = iota((80, 96), 1) & 31
-    same = (inner - 3 * ((inner * 171) >> 9)) == (iota((80, 96), 0) & 7)
-    return jnp.where(same, total, 0.0).astype(bf16)
+        tmp_ref[0:BASIS, 32 * d : 32 * d + BASIS] = high.astype(f32)
+        tmp_ref[24 : 24 + BASIS, 32 * d : 32 * d + BASIS] = low.astype(f32)
+    high_ref[...] = kron8(tmp_ref[0:BASIS, 0:96], expand, diag)
+    low_ref[...] = kron8(tmp_ref[24 : 24 + BASIS, 0:96], expand, diag)
+
+
+def project_weights(proj_ref, tmp_ref, expand, diag, out_ref, packed_ref):
+    for f in range(4):
+        lay(tmp_ref, 16 * f, proj_ref[:, f, :])
+    for f in range(4):
+        out_ref[80 * f : 80 * f + 80] = kron8(tmp_ref[16 * f : 16 * f + FACE, 0:96], expand, diag)
+    row = iota((128, 64), 0)
+    inner = row & 31
+    pick = ones_where((inner < 30) & ((row >> 5) * 16 + third(inner) == iota((128, 64), 1)))
+    rows = dot(pick, tmp_ref[0:64, 0:96].astype(bf16)).astype(bf16)
+    inner = iota((128, 480), 0) & 31
+    same = inner - 3 * third(inner) == (iota((128, 480), 1) & 7)
+    packed_ref[...] = jnp.where(same, dot(rows, expand), 0.0).astype(bf16)
+
+
+def rotate_weights(rot_ref, tmp_ref, expand, diag, out_ref, packed_ref):
+    for o in range(3):
+        lay(tmp_ref, 16 * o, rot_ref[:, o, :])
+    row, col = iota((96, 96), 0), iota((96, 96), 1)
+    inner = col & 31
+    packed = ones_where((inner < 30) & (row >> 5 == col >> 5) & ((row & 31) == third(inner)))
+    inner = iota((8, 96), 1) & 31
+    same = (inner - 3 * third(inner) == iota((8, 96), 0))[None]
+    for o in range(3):
+        rows = tmp_ref[16 * o : 16 * o + FACE, 0:96]
+        out_ref[80 * o : 80 * o + 80] = kron8(rows, expand, diag)
+        packed_ref[80 * o : 80 * o + 80] = kron8(rows, packed, same)
+
+
+def lift_weights(lift_ref, turn_ref, tmp_ref, expand, diag, out_ref):
+    turn_ref[...] = jnp.zeros((128, 128), f32)
+    for f in range(4):
+        turn_ref[16 * f : 16 * f + FACE, 0:BASIS] = lift_ref[:, f, :]
+    lifts = turn_ref[...].T
+    for f in range(4):
+        lay(tmp_ref, 24 * f, -lifts[0:BASIS, 16 * f : 16 * f + FACE])
+    for f in range(4):
+        out_ref[f] = kron8(tmp_ref[24 * f : 24 * f + BASIS, 0:96], expand, diag)
 
 
 def mixed(field, geo, weights):
@@ -146,7 +164,8 @@
 
 def stiff_steps(mix_ref, weights_ref, low_ref, store):
     def step(s):
-        store(s, dot(weights_ref[...], mix_ref[s]) + dot(low_ref[...], mix_ref[s, :480]))
+        high, low = mix_ref[s, :480], mix_ref[s, 480:]
+        store(s, dot(weights_ref[...], high) + dot(weights_ref[...], low) + dot(low_ref[...], high))
 
     return [functools.partial(step, s) for s in range(4)]
 
@@ -159,7 +178,7 @@
 
 def kernel(
     remote,
-    state_ref,
+    state_hbm,
     geo_ref,
     nrm_ref,
     speed_ref,
@@ -177,6 +196,7 @@
     lift_ref,
     rot_ref,
     out_ref,
+    state_ref,
     field_a,
     field_b,
     integral_a,
@@ -194,8 +214,14 @@
     cols_s,
     exp_v,
     exp_s,
-    tmp,
-    tmp2,
+    t0,
+    t1,
+    t2,
+    t3,
+    t4,
+    t5,
+    t6,
+    w_expand,
     w_jac,
     w_stiff_h,
     w_stiff_l,
@@ -211,6 +237,7 @@
     recv_sem,
 ):
     fields, integrals, mixes = (field_a, field_b), (integral_a, integral_b), (mix_a, mix_b)
+    tmps = (t0, t1, t2, t3, t4, t5, t6)
     halves = range(ELEM // WIDE)
 
     links = []
@@ -236,8 +263,13 @@
 
             greeted = greeted + there.astype(i32)
 
+    state_copy = pltpu.make_async_copy(state_hbm, state_ref, cols_sem.at[2])
+    state_copy.start()
+
     index = nbi_ref[...]
-    cols_v[...] = ROWS * jnp.where(index < ELEM, nbf_ref[...] * ELEM + index, 3 * ELEM + index)
+    slots = ROWS * jnp.where(index < ELEM, nbf_ref[...] * ELEM + index, 3 * ELEM + index)
+    for t in range(ELEM // 128):
+        cols_v[:, t, :] = slots[:, 128 * t : 128 * t + 128]
     exp_v[:, 0:256] = ROWS * exs_ref[...]
     exp_v[:, 256:384] = ROWS * exd_ref[...]
     exp_v[:, 384:512] = ROWS * exz_ref[...]
@@ -248,11 +280,13 @@
     for copy in index_copies:
         copy.start()
 
-    jacobian_weights(jac_ref, tmp, w_jac)
-    stiff_weights(stiff_ref, -1.0, w_stiff_h, w_stiff_l)
-    for f in range(4):
-        w_proj[80 * f : 80 * f + 80] = stacked(proj_ref[:, f, :], BASIS)
-        w_proj3[32 * f : 32 * f + 32] = packed_project(proj_ref[:, f, :])
+    expand20, diag20 = expander(BASIS), diagonal(24 * BASIS)
+    for ref in tmps:
+        ref[...] = jnp.zeros((128, 128), f32)
+    jacobian_weights(jac_ref, tmps[0], w_jac)
+    stiff_weights(stiff_ref, -1.0, tmps[1], expand20, diag20, w_stiff_h, w_stiff_l)
+    project_weights(proj_ref, tmps[2], expand20, diag20, w_proj, w_proj3)
+    w_expand[...] = expand20
 
     zeros5 = jnp.zeros((5, WIDE), f32)
 
@@ -271,6 +305,7 @@
         coarse = base * (2.0 ** (degree + 1) - 1.0)
         times[degree] = jnp.broadcast_to(jnp.where(fine, f32(base), f32(coarse)), (8, ELEM))
 
+    state_copy.wait()
     for h in halves:
         for b in range(BASIS):
             value = jnp.concatenate([state_ref[b, :, columns(h)], zeros5], axis=0)
@@ -311,10 +346,10 @@
                     chunk = whole[128 * c : min(128 * c + 128, TRACE), 128 * t : 128 * t + 128]
                     if c == ROWS - 1:
                         chunk = jnp.concatenate([chunk, jnp.zeros((128 - chunk.shape[0], 128), f32)], axis=0)
-                    turned = chunk.T
-                    mine[pl.ds(base + c, 128, stride=ROWS), :] = turned
-                    pool[pl.ds(base + c, 128, stride=ROWS), :] = turned
-
+                    mine[pl.ds(base + c, 128, stride=ROWS), :] = chunk.T
+
+    own_copy = pltpu.make_async_copy(mine, pool.at[pl.ds(0, ROWS * 4 * ELEM), :], cols_sem.at[3])
+    own_copy.start()
     for copy in index_copies:
         copy.wait()
     if remote:
@@ -325,13 +360,9 @@
         side = at % 2
         lane = (0, 256, 384)[at // 2]
 
-        def export(t, carry, side=side, first=first, lane=lane):
-            for u in range(64):
-                row = exp_s[side, lane + t * 64 + u]
-                ship[pl.ds(ROWS * (first + t * 64 + u), ROWS), :] = mine[pl.ds(row, ROWS), :]
-            return carry
-
-        lax.fori_loop(0, rows // 64, export, 0)
+        for n in range(rows):
+            row = exp_s[side, lane + n]
+            ship[pl.ds(ROWS * (first + n), ROWS), :] = mine[pl.ds(row, ROWS), :]
         source = ship.at[pl.ds(ROWS * first, ROWS * rows), :]
         goal = pool.at[pl.ds(ROWS * (4 * ELEM + land), ROWS * rows), :]
         if remote:
@@ -349,16 +380,10 @@
             copy.start()
         copies.append(copy)
 
-    stiff_weights(vol_ref, 1.0, w_vol_h, w_vol_l)
-    tmp2[...] = jnp.zeros((128, 128), f32)
-    for f in range(4):
-        tmp2[16 * f : 16 * f + FACE, 0:BASIS] = lift_ref[:, f, :]
-    lifts = tmp2[...].T
-    for o in range(3):
-        w_rot[80 * o : 80 * o + 80] = stacked(rot_ref[:, o, :], FACE)
-        w_rot3[80 * o : 80 * o + 80] = packed_rotate(rot_ref[:, o, :])
-    for f in range(4):
-        w_lift[f] = stacked(-lifts[0:BASIS, 16 * f : 16 * f + FACE], FACE)
+    stiff_weights(vol_ref, 1.0, tmps[3], w_expand[...], diag20, w_vol_h, w_vol_l)
+    expand10, diag10 = expander(FACE), diagonal(24 * FACE)
+    rotate_weights(rot_ref, tmps[4], expand10, diag10, w_rot, w_rot3)
+    lift_weights(lift_ref, tmps[6], tmps[5], expand10, diag10, w_lift)
 
     phases = [mix_steps(lambda b, h=h: integrals[h][b], geometry(h), w_jac, mixes[h]) for h in halves]
     for h in halves:
@@ -369,6 +394,7 @@
         phases.append(stiff_steps(mixes[h], w_vol_h, w_vol_l, store))
     run(*phases)
 
+    own_copy.wait()
     for at, (axis, there, target, first, land, rows) in enumerate(links):
         copy = copies[at]
         if remote:
@@ -390,7 +416,7 @@
 
     def fetch(f, first, count):
         for n in range(first, first + count):
-            near[pl.ds(ROWS * n, ROWS), :] = pool[pl.ds(cols_s[f, n], ROWS), :]
+            near[pl.ds(ROWS * n, ROWS), :] = pool[pl.ds(cols_s[f, n // 128, n % 128], ROWS), :]
 
     def turned(f, h):
         tiles = []
@@ -463,9 +489,10 @@
     return pl.pallas_call(
         functools.partial(kernel, remote),
         out_shape=pltpu.VMEM((BASIS, QUANT, ELEM), f32),
-        in_specs=[vmem] * 17,
+        in_specs=[pl.BlockSpec(memory_space=pl.ANY)] + [vmem] * 16,
         out_specs=vmem,
         scratch_shapes=[
+            pltpu.VMEM((BASIS, QUANT, ELEM), f32),
             pltpu.VMEM((BASIS, 32, WIDE), f32),
             pltpu.VMEM((BASIS, 32, WIDE), f32),
             pltpu.VMEM((BASIS, 32, WIDE), f32),
@@ -479,23 +506,23 @@
             pltpu.VMEM((ROWS * 6 * ELEM, 128), f32),
             pltpu.VMEM((ROWS * 2 * ELEM, 128), f32),
             pltpu.VMEM((ROWS * ELEM, 128), f32),
-            pltpu.VMEM((4, ELEM), i32),
-            pltpu.SMEM((4, ELEM), i32),
+            pltpu.VMEM((4, 4, 128), i32),
+            pltpu.SMEM((4, 4, 128), i32),
             pltpu.VMEM((2, ELEM), i32),
             pltpu.SMEM((2, ELEM), i32),
-            pltpu.VMEM((128, 128), f32),
-            pltpu.VMEM((128, 128), f32),
+            *[pltpu.VMEM((128, 128), f32)] * 7,
+            pltpu.VMEM((96, 480), bf16),
             pltpu.VMEM((96, 96), bf16),
-            pltpu.VMEM((160, 960), bf16),
             pltpu.VMEM((160, 480), bf16),
-            pltpu.VMEM((160, 960), bf16),
+            pltpu.VMEM((160, 480), bf16),
+            pltpu.VMEM((160, 480), bf16),
             pltpu.VMEM((160, 480), bf16),
             pltpu.VMEM((320, 480), bf16),
             pltpu.VMEM((128, 480), bf16),
             pltpu.VMEM((240, 240), bf16),
             pltpu.VMEM((240, 96), bf16),
             pltpu.VMEM((4, 160, 240), bf16),
-            pltpu.SemaphoreType.DMA((2,)),
+            pltpu.SemaphoreType.DMA((4,)),
             pltpu.SemaphoreType.DMA((6,)),
             pltpu.SemaphoreType.DMA((6,)),
         ],

time: 29.1 us -> 28 us (0.962)
  Pallas kernels: 27.9 us -> 26.8 us
    pallas_call x1, Pallas kernels: 27.9 us -> 26.8 us  [update_call(): pl.pallas_call(functools.partial(kernel, remote), out_shape=pltpu.VMEM((B...]
where the time goes in v2:
time: 28 us; the launch traced here: 27.9 us
  Pallas kernels  26.8 us (96%)
  local copies, waits for them, and re-layouts  1.06 us (4%)
    pallas_call x1, Pallas kernels, update_call(): pl.pallas_call(functools.partial(kernel, remote), out_shape=pltpu.VMEM((B...  26.8 us
    unnamed x1, local copies, waits for them, and re-layouts  1.06 us

profile of v2, /device:TPU:109, one launch (start us, length us, event | category | flops | bytes accessed | tf_op | source)
XLA Modules:
  0.0 27.9 jit_solution(6443336867496310089)
XLA Ops:
  0.0 26.8 %shard_map.163 = f32[20,27,512]{2,1,0:T(8,128)S(1)} custom-call(f32[20,27,512]{2,1,0:T(8,128)} %state_hbm.1, f32[3,3,512]{2,1,0:T(4,128)} %geo_ref.1, f32[3,4,512]{2,1,0:T(4,128)} %bitcast.6, f32[1,512]{1,0:T(1,128)} %bitcast.10, s32[1,512]{1,0:T(1,128)} %bitcast.11, s32[4,512]{1,0:T(4,128)} %nbi_ref.1, s32[4,512]{1,0:T(4,128)} %nbf_ref.1, ...), custom_call_target="tpu_custom_call" | custom-call | tf_op jit(solution)/shard_map/pallas_call | solution.py:489
  26.8 1.1 %copy.19 = f32[20,27,512]{2,1,0:T(8,128)} copy(f32[20,27,512]{2,1,0:T(8,128)S(1)} %shard_map.163) | data formatting | bytes 2211840

commit v3 on v2

--- a/solution.py
+++ b/solution.py
@@ -19,13 +19,18 @@
 f32, bf16, i32 = jnp.float32, jnp.bfloat16, jnp.int32
 
 LINKS = (
-    ("strike", 0, 256),
-    ("strike", 256, 256),
-    ("dip", 512, 128),
-    ("dip", 640, 128),
-    ("depth", 768, 128),
-    ("depth", 896, 128),
+    ("strike", -1, 0, 256, 128),
+    ("strike", 1, 256, 0, 128),
+    ("dip", -1, 512, 640, 128),
+    ("dip", 1, 640, 512, 128),
+    ("depth", -1, 768, 896, 128),
+    ("depth", 1, 896, 768, 128),
+    ("strike", -1, 128, 384, 128),
+    ("strike", 1, 384, 128, 128),
 )
+LANES = {"strike": 0, "dip": 256, "depth": 384}
+STARTS = {"strike": 0, "dip": 512, "depth": 768}
+WIDTHS = {"strike": 256, "dip": 128, "depth": 128}
 
 
 def dot(a, b):
@@ -240,22 +245,20 @@
     tmps = (t0, t1, t2, t3, t4, t5, t6)
     halves = range(ELEM // WIDE)
 
-    links = []
-    for at, (axis, first, rows) in enumerate(LINKS):
-        step = -1 if at % 2 == 0 else 1
-        if remote:
-            pos, count = lax.axis_index(axis), lax.axis_size(axis)
-            there = pos > 0 if step < 0 else pos < count - 1
-            target = jnp.clip(pos + step, 0, count - 1)
-        else:
-            there, target = True, None
-        land = first + rows if step < 0 else first - rows
-        links.append((axis, there, target, first, land, rows))
+    sides = {}
+    for axis in ("strike", "dip", "depth"):
+        for step in (-1, 1):
+            if remote:
+                pos, count = lax.axis_index(axis), lax.axis_size(axis)
+                there = pos > 0 if step < 0 else pos < count - 1
+                sides[axis, step] = there, jnp.clip(pos + step, 0, count - 1)
+            else:
+                sides[axis, step] = True, None
 
     if remote:
         barrier = pltpu.get_barrier_semaphore()
         greeted = 0
-        for axis, there, target, *_ in links:
+        for (axis, step), (there, target) in sides.items():
 
             @pl.when(there)
             def _(axis=axis, target=target):
@@ -328,25 +331,31 @@
 
     lax.fori_loop(1, ORDER, predict, 0)
 
+    def operand(h, s):
+        high, low = split(integrals[h][:, 8 * s : 8 * s + 8, :].reshape(BASIS * 8, WIDE))
+        return jnp.concatenate([high, low, high], axis=0)
+
+    def keep_own(f, h, s, rows):
+        own[f, :, 8 * s : 8 * s + 8, columns(h)] = rows.reshape(FACE, 8, WIDE)
+
     for h in halves:
-        for s in range(4):
-            high, low = split(integrals[h][:, 8 * s : 8 * s + 8, :].reshape(BASIS * 8, WIDE))
-            operand = jnp.concatenate([high, low, high], axis=0)
-            traces = dot(w_proj[...], operand)
-            for f in range(4):
-                own[f, :, 8 * s : 8 * s + 8, columns(h)] = traces[80 * f : 80 * f + 80].reshape(FACE, 8, WIDE)
-            if s == 3:
-                packed = dot(w_proj3[...], operand)
-        for f in range(4):
-            pieces = [own[f, :, 8 * s : 8 * s + 8, columns(h)].reshape(80, WIDE) for s in range(3)]
-            whole = jnp.concatenate(pieces + [packed[32 * f : 32 * f + 32]], axis=0)
-            for t in range(WIDE // 128):
-                base = ROWS * (f * ELEM + h * WIDE + 128 * t)
-                for c in range(ROWS):
-                    chunk = whole[128 * c : min(128 * c + 128, TRACE), 128 * t : 128 * t + 128]
-                    if c == ROWS - 1:
-                        chunk = jnp.concatenate([chunk, jnp.zeros((128 - chunk.shape[0], 128), f32)], axis=0)
-                    mine[pl.ds(base + c, 128, stride=ROWS), :] = chunk.T
+        operands = [operand(h, s) for s in range(4)]
+        packed = dot(w_proj3[...], operands[3])
+        for pair in (0, 2):
+            slabs = [dot(w_proj[80 * pair : 80 * pair + 160], operands[s]) for s in range(3)]
+            for f in (pair, pair + 1):
+                pieces = [slab[80 * (f - pair) : 80 * (f - pair) + 80] for slab in slabs]
+                for s in range(3):
+                    keep_own(f, h, s, pieces[s])
+                whole = jnp.concatenate(pieces + [packed[32 * f : 32 * f + 32]], axis=0)
+                for t in range(WIDE // 128):
+                    base = ROWS * (f * ELEM + h * WIDE + 128 * t)
+                    for c in range(ROWS):
+                        chunk = whole[128 * c : min(128 * c + 128, TRACE), 128 * t : 128 * t + 128]
+                        if c == ROWS - 1:
+                            short = jnp.zeros((128 - chunk.shape[0], 128), f32)
+                            chunk = jnp.concatenate([chunk, short], axis=0)
+                        mine[pl.ds(base + c, 128, stride=ROWS), :] = chunk.T
 
     own_copy = pltpu.make_async_copy(mine, pool.at[pl.ds(0, ROWS * 4 * ELEM), :], cols_sem.at[3])
     own_copy.start()
@@ -355,31 +364,36 @@
     if remote:
         pl.semaphore_wait(barrier, greeted)
 
-    copies = []
-    for at, (axis, there, target, first, land, rows) in enumerate(links):
-        side = at % 2
-        lane = (0, 256, 384)[at // 2]
-
+    def link(at):
+        axis, step, first, land, rows = LINKS[at]
+        source = ship.at[pl.ds(ROWS * first, ROWS * rows), :]
+        goal = pool.at[pl.ds(ROWS * (4 * ELEM + land), ROWS * rows), :]
+        if not remote:
+            return pltpu.make_async_copy(source, goal, send_sem.at[at])
+        return pltpu.make_async_remote_copy(
+            src_ref=source,
+            dst_ref=goal,
+            send_sem=send_sem.at[at],
+            recv_sem=recv_sem.at[at],
+            device_id={axis: sides[axis, step][1]},
+            device_id_type=MESH,
+        )
+
+    for at, (axis, step, first, land, rows) in enumerate(LINKS):
+        side = 0 if step < 0 else 1
+        lane = LANES[axis] + first - STARTS[axis] - side * WIDTHS[axis]
         for n in range(rows):
             row = exp_s[side, lane + n]
             ship[pl.ds(ROWS * (first + n), ROWS), :] = mine[pl.ds(row, ROWS), :]
-        source = ship.at[pl.ds(ROWS * first, ROWS * rows), :]
-        goal = pool.at[pl.ds(ROWS * (4 * ELEM + land), ROWS * rows), :]
         if remote:
-            copy = pltpu.make_async_remote_copy(
-                src_ref=source,
-                dst_ref=goal,
-                send_sem=send_sem.at[at],
-                recv_sem=recv_sem.at[at ^ 1],
-                device_id={axis: target},
-                device_id_type=MESH,
-            )
-            pl.when(there)(copy.start)
+            pl.when(sides[axis, step][0])(link(at).start)
         else:
-            copy = pltpu.make_async_copy(source, goal, send_sem.at[at])
-            copy.start()
-        copies.append(copy)
-
+            link(at).start()
+
+    for h in halves:
+        rows = dot(w_proj[...], operand(h, 3))
+        for f in range(4):
+            keep_own(f, h, 3, rows[80 * f : 80 * f + 80])
     stiff_weights(vol_ref, 1.0, tmps[3], w_expand[...], diag20, w_vol_h, w_vol_l)
     expand10, diag10 = expander(FACE), diagonal(24 * FACE)
     rotate_weights(rot_ref, tmps[4], expand10, diag10, w_rot, w_rot3)
@@ -395,22 +409,11 @@
     run(*phases)
 
     own_copy.wait()
-    for at, (axis, there, target, first, land, rows) in enumerate(links):
-        copy = copies[at]
+    for at, (axis, step, *_) in enumerate(LINKS):
+        copy = link(at)
         if remote:
-            arrived = pltpu.make_async_remote_copy(
-                src_ref=ship.at[pl.ds(ROWS * first, ROWS * rows), :],
-                dst_ref=pool.at[pl.ds(ROWS * (4 * ELEM + first), ROWS * rows), :],
-                send_sem=send_sem.at[at],
-                recv_sem=recv_sem.at[at],
-                device_id={axis: target},
-                device_id_type=MESH,
-            )
-
-            @pl.when(there)
-            def _(copy=copy, arrived=arrived):
-                copy.wait_send()
-                arrived.wait_recv()
+            pl.when(sides[axis, step][0])(copy.wait_send)
+            pl.when(sides[axis, -step][0])(copy.wait_recv)
         else:
             copy.wait()
 
@@ -425,7 +428,7 @@
             parts = [near[pl.ds(base + c, 128, stride=ROWS), :].T for c in range(ROWS)]
             tiles.append(jnp.concatenate([parts[0], parts[1], parts[2][: TRACE - 256]], axis=0))
         high, low = split(jnp.concatenate(tiles, axis=1))
-        turn = jnp.broadcast_to(orient_ref[pl.ds(f, 1), columns(h)], (8, WIDE))[None]
+        turn = jnp.broadcast_to(orient_ref[f : f + 1, columns(h)], (8, WIDE))[None]
         slabs = []
         for s in range(4):
             rows = slice(80 * s, min(80 * s + 80, TRACE))
@@ -436,7 +439,7 @@
 
     def fluxes(f, h, slabs):
         normal = [
-            0.5 * jnp.broadcast_to(nrm_ref[j, pl.ds(f, 1), columns(h)], (8, WIDE))[None] for j in range(3)
+            0.5 * jnp.broadcast_to(nrm_ref[j, f : f + 1, columns(h)], (8, WIDE))[None] for j in range(3)
         ]
         speed = 0.5 * jnp.broadcast_to(speed_ref[:, columns(h)], (8, WIDE))[None]
         flux = []
@@ -458,20 +461,19 @@
             total[s, :, columns(h)] += dot(w_lift[f], operand)
 
     fetch(0, 0, ELEM)
-
-    def faces(f, carry):
-        later = jnp.minimum(f + 1, 3)
-        slabs = [turned(f, h) for h in halves]
-        flux = []
+    slabs = [turned(0, h) for h in halves]
+    fetch(1, 0, ELEM)
+    for f in range(4):
+        flux, later = [], []
         for h in halves:
+            if f < 3:
+                later.append(turned(f + 1, h))
             flux.append(fluxes(f, h, slabs[h]))
-            fetch(later, h * (ELEM // 4), ELEM // 4)
         for h in halves:
             lifted(f, h, flux[h])
-            fetch(later, ELEM // 2 + h * (ELEM // 4), ELEM // 4)
-        return carry
-
-    lax.fori_loop(0, 4, faces, 0)
+            if f < 2:
+                fetch(f + 2, h * (ELEM // 2), ELEM // 2)
+        slabs = later
 
     for h in halves:
         keep = jnp.broadcast_to(cluster_ref[:, columns(h)], (8, WIDE)) == 0
@@ -523,8 +525,8 @@
             pltpu.VMEM((240, 96), bf16),
             pltpu.VMEM((4, 160, 240), bf16),
             pltpu.SemaphoreType.DMA((4,)),
-            pltpu.SemaphoreType.DMA((6,)),
-            pltpu.SemaphoreType.DMA((6,)),
+            pltpu.SemaphoreType.DMA((8,)),
+            pltpu.SemaphoreType.DMA((8,)),
         ],
         compiler_params=pltpu.CompilerParams(
             vmem_limit_bytes=56 * 2**20,

time: 28 us -> 26.9 us (0.961)
  Pallas kernels: 26.8 us -> 25.6 us
    pallas_call x1, Pallas kernels: 26.8 us -> 25.6 us  [update_call(): pl.pallas_call(functools.partial(kernel, remote), out_shape=pltpu.VMEM((B...]
where the time goes in v3:
time: 26.9 us; the launch traced here: 26.7 us
  Pallas kernels  25.6 us (95%)
  local copies, waits for them, and re-layouts  1.06 us (4%)
    pallas_call x1, Pallas kernels, update_call(): pl.pallas_call(functools.partial(kernel, remote), out_shape=pltpu.VMEM((B...  25.6 us
    unnamed x1, local copies, waits for them, and re-layouts  1.06 us

profile of v3, /device:TPU:109, one launch (start us, length us, event | category | flops | bytes accessed | tf_op | source)
XLA Modules:
  0.0 26.7 jit_solution(1564428683345541463)
XLA Ops:
  0.0 25.6 %shard_map.163 = f32[20,27,512]{2,1,0:T(8,128)S(1)} custom-call(f32[20,27,512]{2,1,0:T(8,128)} %state_hbm.1, f32[3,3,512]{2,1,0:T(4,128)} %geo_ref.1, f32[3,4,512]{2,1,0:T(4,128)} %bitcast.6, f32[1,512]{1,0:T(1,128)} %bitcast.10, s32[1,512]{1,0:T(1,128)} %bitcast.11, s32[4,512]{1,0:T(4,128)} %nbi_ref.1, s32[4,512]{1,0:T(4,128)} %nbf_ref.1, ...), custom_call_target="tpu_custom_call" | custom-call | tf_op jit(solution)/shard_map/pallas_call | solution.py:491
  25.6 1.1 %copy.19 = f32[20,27,512]{2,1,0:T(8,128)} copy(f32[20,27,512]{2,1,0:T(8,128)S(1)} %shard_map.163) | data formatting | bytes 2211840

commit v4 on v3

--- a/solution.py
+++ b/solution.py
@@ -16,17 +16,19 @@
 WIDE = 256
 ROWS = 3
 TRACE = 272
+LINK = 128
+PARCEL = 2 * LINK + LINK // 8
 f32, bf16, i32 = jnp.float32, jnp.bfloat16, jnp.int32
 
 LINKS = (
-    ("strike", -1, 0, 256, 128),
-    ("strike", 1, 256, 0, 128),
-    ("dip", -1, 512, 640, 128),
-    ("dip", 1, 640, 512, 128),
-    ("depth", -1, 768, 896, 128),
-    ("depth", 1, 896, 768, 128),
-    ("strike", -1, 128, 384, 128),
-    ("strike", 1, 384, 128, 128),
+    ("strike", -1, 0, 256),
+    ("strike", 1, 256, 0),
+    ("dip", -1, 512, 640),
+    ("dip", 1, 640, 512),
+    ("depth", -1, 768, 896),
+    ("depth", 1, 896, 768),
+    ("strike", -1, 128, 384),
+    ("strike", 1, 384, 128),
 )
 LANES = {"strike": 0, "dip": 256, "depth": 384}
 STARTS = {"strike": 0, "dip": 512, "depth": 768}
@@ -211,9 +213,10 @@
     times,
     own,
     total,
-    mine,
     pool,
     ship,
+    thirds,
+    arrive,
     near,
     cols_v,
     cols_s,
@@ -355,19 +358,16 @@
                         if c == ROWS - 1:
                             short = jnp.zeros((128 - chunk.shape[0], 128), f32)
                             chunk = jnp.concatenate([chunk, short], axis=0)
-                        mine[pl.ds(base + c, 128, stride=ROWS), :] = chunk.T
-
-    own_copy = pltpu.make_async_copy(mine, pool.at[pl.ds(0, ROWS * 4 * ELEM), :], cols_sem.at[3])
-    own_copy.start()
+                        pool[pl.ds(base + c, 128, stride=ROWS), :] = chunk.T
+
     for copy in index_copies:
         copy.wait()
     if remote:
         pl.semaphore_wait(barrier, greeted)
 
     def link(at):
-        axis, step, first, land, rows = LINKS[at]
-        source = ship.at[pl.ds(ROWS * first, ROWS * rows), :]
-        goal = pool.at[pl.ds(ROWS * (4 * ELEM + land), ROWS * rows), :]
+        axis, step = LINKS[at][:2]
+        source, goal = (ref.at[pl.ds(PARCEL * at, PARCEL), :] for ref in (ship, arrive))
         if not remote:
             return pltpu.make_async_copy(source, goal, send_sem.at[at])
         return pltpu.make_async_remote_copy(
@@ -379,16 +379,30 @@
             device_id_type=MESH,
         )
 
-    for at, (axis, step, first, land, rows) in enumerate(LINKS):
+    for at, (axis, step, first, land) in enumerate(LINKS):
         side = 0 if step < 0 else 1
         lane = LANES[axis] + first - STARTS[axis] - side * WIDTHS[axis]
-        for n in range(rows):
-            row = exp_s[side, lane + n]
-            ship[pl.ds(ROWS * (first + n), ROWS), :] = mine[pl.ds(row, ROWS), :]
+        for n in range(LINK):
+            rows = pool[pl.ds(exp_s[side, lane + n], ROWS), :]
+            ship[pl.ds(PARCEL * at + 2 * n, 2), :] = rows[0:2]
+            thirds[pl.ds(LINK * at + n, 1), :] = rows[2:3]
+        packed = thirds[LINK * at : LINK * at + 16, :]
+        for k in range(1, 8):
+            packed = packed + pltpu.roll(thirds[LINK * at + 16 * k : LINK * at + 16 * k + 16, :], 16 * k, 1)
+        ship[PARCEL * at + 2 * LINK : PARCEL * (at + 1), :] = packed
         if remote:
             pl.when(sides[axis, step][0])(link(at).start)
         else:
             link(at).start()
+
+    def unpack(at):
+        base = ROWS * (4 * ELEM + LINKS[at][3])
+        for c in range(2):
+            pool[pl.ds(base + c, LINK, stride=ROWS), :] = arrive[pl.ds(PARCEL * at + c, LINK, stride=2), :]
+        packed = arrive[PARCEL * at + 2 * LINK : PARCEL * (at + 1), :]
+        for k in range(8):
+            rows = packed if k == 0 else pltpu.roll(packed, 128 - 16 * k, 1)
+            pool[pl.ds(base + ROWS * 16 * k + 2, 16, stride=ROWS), :] = rows
 
     for h in halves:
         rows = dot(w_proj[...], operand(h, 3))
@@ -408,14 +422,19 @@
         phases.append(stiff_steps(mixes[h], w_vol_h, w_vol_l, store))
     run(*phases)
 
-    own_copy.wait()
     for at, (axis, step, *_) in enumerate(LINKS):
-        copy = link(at)
         if remote:
-            pl.when(sides[axis, step][0])(copy.wait_send)
-            pl.when(sides[axis, -step][0])(copy.wait_recv)
+            @pl.when(sides[axis, -step][0])
+            def _(at=at):
+                link(at).wait_recv()
+                unpack(at)
+
         else:
-            copy.wait()
+            link(at).wait()
+            unpack(at)
+    if remote:
+        for at, (axis, step, *_) in enumerate(LINKS):
+            pl.when(sides[axis, step][0])(link(at).wait_send)
 
     def fetch(f, first, count):
         for n in range(first, first + count):
@@ -504,9 +523,10 @@
             pltpu.VMEM((ORDER, 8, ELEM), f32),
             pltpu.VMEM((4, FACE, 32, ELEM), f32),
             pltpu.VMEM((4, 160, ELEM), f32),
-            pltpu.VMEM((ROWS * 4 * ELEM, 128), f32),
             pltpu.VMEM((ROWS * 6 * ELEM, 128), f32),
-            pltpu.VMEM((ROWS * 2 * ELEM, 128), f32),
+            pltpu.VMEM((PARCEL * len(LINKS), 128), f32),
+            pltpu.VMEM((LINK * len(LINKS), 128), f32),
+            pltpu.VMEM((PARCEL * len(LINKS), 128), f32),
             pltpu.VMEM((ROWS * ELEM, 128), f32),
             pltpu.VMEM((4, 4, 128), i32),
             pltpu.SMEM((4, 4, 128), i32),
@@ -524,7 +544,7 @@
             pltpu.VMEM((240, 240), bf16),
             pltpu.VMEM((240, 96), bf16),
             pltpu.VMEM((4, 160, 240), bf16),
-            pltpu.SemaphoreType.DMA((4,)),
+            pltpu.SemaphoreType.DMA((3,)),
             pltpu.SemaphoreType.DMA((8,)),
             pltpu.SemaphoreType.DMA((8,)),
         ],

time: 26.9 us -> 25.9 us (0.963)
  Pallas kernels: 25.6 us -> 24.6 us
    pallas_call x1, Pallas kernels: 25.6 us -> 24.6 us  [update_call(): pl.pallas_call(functools.partial(kernel, remote), out_shape=pltpu.VMEM((B...]
where the time goes in v4:
time: 25.9 us; the launch traced here: 25.7 us
  Pallas kernels  24.6 us (95%)
  local copies, waits for them, and re-layouts  1.06 us (4%)
    pallas_call x1, Pallas kernels, update_call(): pl.pallas_call(functools.partial(kernel, remote), out_shape=pltpu.VMEM((B...  24.6 us
    unnamed x1, local copies, waits for them, and re-layouts  1.06 us

profile of v4, /device:TPU:109, one launch (start us, length us, event | category | flops | bytes accessed | tf_op | source)
XLA Modules:
  0.0 25.7 jit_solution(1639451718896646122)
XLA Ops:
  0.0 24.6 %shard_map.163 = f32[20,27,512]{2,1,0:T(8,128)S(1)} custom-call(f32[20,27,512]{2,1,0:T(8,128)} %state_hbm.1, f32[3,3,512]{2,1,0:T(4,128)} %geo_ref.1, f32[3,4,512]{2,1,0:T(4,128)} %bitcast.6, f32[1,512]{1,0:T(1,128)} %bitcast.10, s32[1,512]{1,0:T(1,128)} %bitcast.11, s32[4,512]{1,0:T(4,128)} %nbi_ref.1, s32[4,512]{1,0:T(4,128)} %nbf_ref.1, ...), custom_call_target="tpu_custom_call" | custom-call | tf_op jit(solution)/shard_map/pallas_call | solution.py:510
  24.6 1.1 %copy.19 = f32[20,27,512]{2,1,0:T(8,128)} copy(f32[20,27,512]{2,1,0:T(8,128)S(1)} %shard_map.163) | data formatting | bytes 2211840

commit v5 on v4

--- a/solution.py
+++ b/solution.py
@@ -215,7 +215,7 @@
     total,
     pool,
     ship,
-    thirds,
+    taken,
     arrive,
     near,
     cols_v,
@@ -383,12 +383,15 @@
         side = 0 if step < 0 else 1
         lane = LANES[axis] + first - STARTS[axis] - side * WIDTHS[axis]
         for n in range(LINK):
-            rows = pool[pl.ds(exp_s[side, lane + n], ROWS), :]
-            ship[pl.ds(PARCEL * at + 2 * n, 2), :] = rows[0:2]
-            thirds[pl.ds(LINK * at + n, 1), :] = rows[2:3]
-        packed = thirds[LINK * at : LINK * at + 16, :]
+            taken[pl.ds(ROWS * (LINK * at + n), ROWS), :] = pool[pl.ds(exp_s[side, lane + n], ROWS), :]
+        base = ROWS * LINK * at
+        for c in range(2):
+            ship[PARCEL * at + c * LINK : PARCEL * at + (c + 1) * LINK, :] = taken[
+                pl.ds(base + c, LINK, stride=ROWS), :
+            ]
+        packed = taken[pl.ds(base + 2, 16, stride=ROWS), :]
         for k in range(1, 8):
-            packed = packed + pltpu.roll(thirds[LINK * at + 16 * k : LINK * at + 16 * k + 16, :], 16 * k, 1)
+            packed = packed + pltpu.roll(taken[pl.ds(base + ROWS * 16 * k + 2, 16, stride=ROWS), :], 16 * k, 1)
         ship[PARCEL * at + 2 * LINK : PARCEL * (at + 1), :] = packed
         if remote:
             pl.when(sides[axis, step][0])(link(at).start)
@@ -398,7 +401,9 @@
     def unpack(at):
         base = ROWS * (4 * ELEM + LINKS[at][3])
         for c in range(2):
-            pool[pl.ds(base + c, LINK, stride=ROWS), :] = arrive[pl.ds(PARCEL * at + c, LINK, stride=2), :]
+            pool[pl.ds(base + c, LINK, stride=ROWS), :] = arrive[
+                PARCEL * at + c * LINK : PARCEL * at + (c + 1) * LINK, :
+            ]
         packed = arrive[PARCEL * at + 2 * LINK : PARCEL * (at + 1), :]
         for k in range(8):
             rows = packed if k == 0 else pltpu.roll(packed, 128 - 16 * k, 1)
@@ -444,8 +449,10 @@
         tiles = []
         for t in range(WIDE // 128):
             base = ROWS * (h * WIDE + 128 * t)
-            parts = [near[pl.ds(base + c, 128, stride=ROWS), :].T for c in range(ROWS)]
-            tiles.append(jnp.concatenate([parts[0], parts[1], parts[2][: TRACE - 256]], axis=0))
+            parts = [near[pl.ds(base + c, 128, stride=ROWS), :] for c in range(ROWS)]
+            tiles.append(
+                jnp.concatenate([parts[0].T, parts[1].T, parts[2][:, : TRACE - 256].T], axis=0)
+            )
         high, low = split(jnp.concatenate(tiles, axis=1))
         turn = jnp.broadcast_to(orient_ref[f : f + 1, columns(h)], (8, WIDE))[None]
         slabs = []
@@ -525,7 +532,7 @@
             pltpu.VMEM((4, 160, ELEM), f32),
             pltpu.VMEM((ROWS * 6 * ELEM, 128), f32),
             pltpu.VMEM((PARCEL * len(LINKS), 128), f32),
-            pltpu.VMEM((LINK * len(LINKS), 128), f32),
+            pltpu.VMEM((ROWS * LINK * len(LINKS), 128), f32),
             pltpu.VMEM((PARCEL * len(LINKS), 128), f32),
             pltpu.VMEM((ROWS * ELEM, 128), f32),
             pltpu.VMEM((4, 4, 128), i32),

time: 25.9 us -> 25.8 us (level)
  no operation moved by 1% of the time
where the time goes in v5:
time: 25.8 us; the launch traced here: 25.6 us
  Pallas kernels  24.5 us (95%)
  local copies, waits for them, and re-layouts  1.06 us (4%)
    pallas_call x1, Pallas kernels, update_call(): pl.pallas_call(functools.partial(kernel, remote), out_shape=pltpu.VMEM((B...  24.5 us
    unnamed x1, local copies, waits for them, and re-layouts  1.06 us

profile of v5, /device:TPU:109, one launch (start us, length us, event | category | flops | bytes accessed | tf_op | source)
XLA Modules:
  0.0 25.6 jit_solution(2469409119664640683)
XLA Ops:
  0.0 24.5 %shard_map.163 = f32[20,27,512]{2,1,0:T(8,128)S(1)} custom-call(f32[20,27,512]{2,1,0:T(8,128)} %state_hbm.1, f32[3,3,512]{2,1,0:T(4,128)} %geo_ref.1, f32[3,4,512]{2,1,0:T(4,128)} %bitcast.6, f32[1,512]{1,0:T(1,128)} %bitcast.10, s32[1,512]{1,0:T(1,128)} %bitcast.11, s32[4,512]{1,0:T(4,128)} %nbi_ref.1, s32[4,512]{1,0:T(4,128)} %nbf_ref.1, ...), custom_call_target="tpu_custom_call" | custom-call | tf_op jit(solution)/shard_map/pallas_call | solution.py:517
  24.5 1.1 %copy.19 = f32[20,27,512]{2,1,0:T(8,128)} copy(f32[20,27,512]{2,1,0:T(8,128)S(1)} %shard_map.163) | data formatting | bytes 2211840

commit v6 on v5

--- a/solution.py
+++ b/solution.py
@@ -23,12 +23,12 @@
 LINKS = (
     ("strike", -1, 0, 256),
     ("strike", 1, 256, 0),
+    ("strike", -1, 128, 384),
+    ("strike", 1, 384, 128),
     ("dip", -1, 512, 640),
     ("dip", 1, 640, 512),
     ("depth", -1, 768, 896),
     ("depth", 1, 896, 768),
-    ("strike", -1, 128, 384),
-    ("strike", 1, 384, 128),
 )
 LANES = {"strike": 0, "dip": 256, "depth": 384}
 STARTS = {"strike": 0, "dip": 512, "depth": 768}

time: 25.8 us -> 26.2 us (1.016)
  Pallas kernels: 24.5 us -> 24.9 us
    pallas_call x1, Pallas kernels: 24.5 us -> 24.9 us  [update_call(): pl.pallas_call(functools.partial(kernel, remote), out_shape=pltpu.VMEM((B...]
where the time goes in v6:
time: 26.2 us; the launch traced here: 26 us
  Pallas kernels  24.9 us (95%)
  local copies, waits for them, and re-layouts  1.06 us (4%)
    pallas_call x1, Pallas kernels, update_call(): pl.pallas_call(functools.partial(kernel, remote), out_shape=pltpu.VMEM((B...  24.9 us
    unnamed x1, local copies, waits for them, and re-layouts  1.06 us

profile of v6, /device:TPU:109, one launch (start us, length us, event | category | flops | bytes accessed | tf_op | source)
XLA Modules:
  0.0 26.0 jit_solution(17537845798669013850)
XLA Ops:
  0.0 24.9 %shard_map.163 = f32[20,27,512]{2,1,0:T(8,128)S(1)} custom-call(f32[20,27,512]{2,1,0:T(8,128)} %state_hbm.1, f32[3,3,512]{2,1,0:T(4,128)} %geo_ref.1, f32[3,4,512]{2,1,0:T(4,128)} %bitcast.6, f32[1,512]{1,0:T(1,128)} %bitcast.10, s32[1,512]{1,0:T(1,128)} %bitcast.11, s32[4,512]{1,0:T(4,128)} %nbi_ref.1, s32[4,512]{1,0:T(4,128)} %nbf_ref.1, ...), custom_call_target="tpu_custom_call" | custom-call | tf_op jit(solution)/shard_map/pallas_call | solution.py:517
  24.9 1.1 %copy.19 = f32[20,27,512]{2,1,0:T(8,128)} copy(f32[20,27,512]{2,1,0:T(8,128)S(1)} %shard_map.163) | data formatting | bytes 2211840
